TPU v7x, 128 devices: a whole 4x4x4 slice. The times are simulated.
128 devices in a mesh: row: 16 (over z, x), col: 8 (over y, core).
Axes of the slice: x: 4, y: 4, z: 4, core: 2. Of those that a mesh axis runs over, the one named last changes fastest.
Arguments:
- right_sides: bfloat16 [31, 2432, 256], P(None, ('row', 'col')), may hold values from -6 to 6
- lower_inv: bfloat16 [31, 2432, 2432], P(None, 'col', 'row'), as said below
- lower_off: bfloat16 [98, 2432, 2432], P(None, 'row', 'col'), may hold values from -0.0625 to 0.0625
- upper_inv: bfloat16 [31, 2432, 2432], P(None, 'row', 'col'), as said below
- upper_off: bfloat16 [98, 2432, 2432], P(None, 'col', 'row'), may hold values from -0.0625 to 0.0625
- present: int32 [98], replicated, may hold values 0 or 1
Outputs:
- solution: float32 [31, 2432, 256], P(None, ('row', 'col'))
Inputs may be any that keep to these rules, and one draw needn't show every extreme that they name: `lower_inv`: each block is unit lower triangular. `upper_inv`: each block is upper triangular with a positive diagonal.
All inputs are finite; a program needn't handle non-finite values.
Results may differ from a plain program's by a relative error of at most 0.034.
Values may be sent and summed in bfloat16 or wider, within the bound.
A program may use at most 128 MiB of HBM per device.

v0:
```python
import jax
import jax.numpy as jnp
from jax import lax
from jax.sharding import PartitionSpec as P

LEVELS = 5
R = 256


def level_layout():
    first_nodes = []
    first_blocks = []
    node_total = 0
    block_total = 0
    for height in range(LEVELS):
        members = 2 ** (LEVELS - 1 - height)
        first_nodes.append(node_total)
        first_blocks.append(block_total)
        node_total += members
        block_total += members * (LEVELS - 1 - height)
    return (first_nodes, first_blocks)


def on_device(right_sides, lower_inv, lower_off, upper_inv, upper_off, present):
    first_nodes, first_blocks = level_layout()
    block_scale = present.astype(jnp.float32)
    wide_r = lower_off.shape[1]
    waiting_nodes = [None] * LEVELS
    forward = [None] * LEVELS
    for height in range(LEVELS):
        members = 2 ** (LEVELS - 1 - height)
        first_node = first_nodes[height]
        ancestors = LEVELS - 1 - height
        target = right_sides[first_node : first_node + members].astype(jnp.float32)
        if waiting_nodes[height] is not None:
            target = target - lax.psum_scatter(
                waiting_nodes[height], "col", scatter_dimension=1, tiled=True
            )
        lowered = lax.all_gather(target.astype(jnp.bfloat16), "col", axis=1, tiled=True)
        partial_value = jnp.einsum(
            "oal,olp->oap",
            lower_inv[first_node : first_node + members],
            lowered,
            preferred_element_type=jnp.float32,
        )
        solved_part = lax.psum_scatter(partial_value, "row", scatter_dimension=1, tiled=True)
        forward[height] = solved_part
        spread_factor = None
        if ancestors > 0:
            spread_factor = lax.all_gather(
                solved_part.astype(jnp.bfloat16), "row", axis=1, tiled=True
            )
        for tree_distance in range(1, ancestors + 1):
            start_block = first_blocks[height] + tree_distance - 1
            stop_block = first_blocks[height] + members * ancestors
            block_list = lower_off[start_block:stop_block:ancestors]
            weights = block_scale[start_block:stop_block:ancestors]
            moving = (
                jnp.einsum(
                    "oal,olp->oap", block_list, spread_factor, preferred_element_type=jnp.float32
                )
                * weights[:, None, None]
            )
            grouped = moving.reshape(members >> tree_distance, 2**tree_distance, wide_r, R).sum(
                axis=1
            )
            if waiting_nodes[height + tree_distance] is None:
                waiting_nodes[height + tree_distance] = grouped
            else:
                waiting_nodes[height + tree_distance] = (
                    waiting_nodes[height + tree_distance] + grouped
                )
    upward = [None] * LEVELS
    results = [None] * LEVELS
    for height in reversed(range(LEVELS)):
        members = 2 ** (LEVELS - 1 - height)
        first_node = first_nodes[height]
        target = forward[height]
        if upward[height] is not None:
            target = target - lax.psum_scatter(
                upward[height].astype(jnp.bfloat16), "row", scatter_dimension=1, tiled=True
            ).astype(jnp.float32)
        raised = lax.all_gather(target.astype(jnp.bfloat16), "row", axis=1, tiled=True)
        partial_value = jnp.einsum(
            "oal,olp->oap",
            upper_inv[first_node : first_node + members],
            raised,
            preferred_element_type=jnp.float32,
        )
        solved_part = lax.psum_scatter(
            partial_value.astype(jnp.bfloat16), "col", scatter_dimension=1, tiled=True
        ).astype(jnp.float32)
        results[height] = solved_part
        spread_factor = None
        if height > 0:
            spread_factor = lax.all_gather(
                solved_part.astype(jnp.bfloat16), "col", axis=1, tiled=True
            )
        for tree_distance in range(1, height + 1):
            lower_height = height - tree_distance
            lower_members = members << tree_distance
            lower_above = LEVELS - 1 - lower_height
            start_block = first_blocks[lower_height] + tree_distance - 1
            stop_block = first_blocks[lower_height] + lower_members * lower_above
            block_list = upper_off[start_block:stop_block:lower_above]
            weights = block_scale[start_block:stop_block:lower_above]
            repeated_copies = jnp.repeat(spread_factor, 2**tree_distance, axis=0)
            moving = (
                jnp.einsum(
                    "oal,olp->oap", block_list, repeated_copies, preferred_element_type=jnp.float32
                )
                * weights[:, None, None]
            )
            if upward[lower_height] is None:
                upward[lower_height] = moving
            else:
                upward[lower_height] = upward[lower_height] + moving
    return jnp.concatenate(results, axis=0)


def solution(mesh):
    placed = (
        P(None, ("row", "col"), None),
        P(None, "col", "row"),
        P(None, "row", "col"),
        P(None, "row", "col"),
        P(None, "col", "row"),
        P(),
    )
    return jax.shard_map(
        on_device,
        mesh=mesh,
        in_specs=placed,
        out_specs=P(None, ("row", "col"), None),
        check_vma=False,
    )
```

profile of v0, /device:TPU:1, one launch (start us, length us, event | category | flops | bytes accessed | tf_op | source)
XLA Modules:
  0.0 1660.6 jit_solution(16297274554371626182)
XLA Ops:
  6.5 1.6 slice.146
  8.2 28.3 %all-gather.6.cloned.1.call-done = bf16[16,152,256]{2,0,1:T(8,128)(2,1)} async-done(((bf16[16,19,256]{2,0,1:T(8,128)(2,1)}), bf16[16,152,256]{2,0,1:T(8,128)(2,1)}) %all-gather.6.cloned.1.call-update) | async-done | bytes 1245200 | tf_op jit(solution)/shard_map/all_gather | solution.py:39
  36.5 3.1 fusion.50
  39.6 5.1 copy.99
  44.7 76.9 %reduce-scatter.25.cloned.1.call-done = f32[16,19,256]{2,0,1:T(8,128)} async-done(((f32[16,304,256]{2,0,1:T(8,128)}), f32[16,19,256]{2,0,1:T(8,128)}) %reduce-scatter.25.cloned.1.call-update) | async-done | bytes 311312
  121.6 1.6 convert_element_type.130
  123.4 46.7 %all-gather.8.cloned.1.call-done = bf16[16,304,256]{2,0,1:T(8,128)(2,1)} async-done(((bf16[16,19,256]{2,0,1:T(8,128)(2,1)}), bf16[16,304,256]{2,0,1:T(8,128)(2,1)}) %all-gather.8.cloned.1.call-update) | async-done | bytes 2490384 | tf_op jit(solution)/shard_map/all_gather | solution.py:50
  170.1 3.5 bitcast_reduce_fusion.2
  175.1 29.3 %reduce-scatter.19.cloned.1.call-done = f32[8,19,256]{2,0,1:T(8,128)} async-done(((f32[8,152,256]{2,0,1:T(8,128)}), f32[8,19,256]{2,0,1:T(8,128)}) %reduce-scatter.19.cloned.1.call-update) | async-done | bytes 155664 | tf_op jit(solution)/shard_map/reduce_scatter | solution.py:36
  205.3 16.6 all_gather.58
  221.9 1.8 convolution_bitcast_fusion
  223.6 2.9 copy.104
  226.6 72.8 %reduce-scatter.27.cloned.1.call-done = f32[8,19,256]{2,0,1:T(8,128)} async-done(((f32[8,304,256]{2,0,1:T(8,128)}), f32[8,19,256]{2,0,1:T(8,128)}) %reduce-scatter.27.cloned.1.call-update) | async-done | bytes 155664
  299.5 1.6 convert_element_type.134
  301.3 3.4 bitcast_reduce_fusion.1
  304.7 39.4 %all-gather.10.cloned.1.call-done = bf16[8,304,256]{2,0,1:T(8,128)(2,1)} async-done(((bf16[8,19,256]{2,0,1:T(8,128)(2,1)}), bf16[8,304,256]{2,0,1:T(8,128)(2,1)}) %all-gather.10.cloned.1.call-update) | async-done | bytes 1245200 | tf_op jit(solution)/shard_map/all_gather | solution.py:50
  344.1 2.1 bitcast_reduce_fusion.4
  348.8 58.3 %all-reduce.27.cloned.1.call-done = f32[4,152,256]{2,0,1:T(4,128)} async-done(((f32[4,152,256]{2,0,1:T(4,128)}), f32[4,152,256]{2,0,1:T(4,128)}) %all-reduce.27.cloned.1.call-update) | async-done | bytes 622608
  408.0 16.4 all_gather.60
  425.9 1.9 copy.110
  429.4 3.5 bitcast_reduce_fusion
  432.9 1.7 bitcast_reduce_fusion.3
  434.6 78.7 %all-reduce.29.cloned.1.call-done = f32[4,304,256]{2,0,1:T(4,128)} async-done(((f32[4,304,256]{2,0,1:T(4,128)}), f32[4,304,256]{2,0,1:T(4,128)}) %all-reduce.29.cloned.1.call-update) | async-done | bytes 1245200
  514.3 17.5 %all_gather.61 = bf16[4,304,256]{2,0,1:T(4,128)(2,1)S(1)} all-gather(bf16[4,19,256]{2,0,1:T(4,128)(2,1)S(1)} %dynamic-slice_convert_fusion), channel_id=1, replica_groups=mesh['row'=16,'col'=8] {'row'}, dimensions={1}, use_global_device_ids=true | all-gather | bytes 661504 | tf_op jit(solution)/shard_map/all_gather | solution.py:50
  534.5 63.3 %all-reduce.31.cloned.1.call-done = f32[2,152,256]{2,0,1:T(2,128)} async-done(((f32[2,152,256]{2,0,1:T(2,128)}), f32[2,152,256]{2,0,1:T(2,128)}) %all-reduce.31.cloned.1.call-update) | async-done | bytes 311312
  598.6 15.7 all_gather.62
  617.0 3.4 multiply_reduce_fusion
  620.4 1.7 fusion.46
  623.5 76.8 %all-reduce.33.cloned.1.call-done = f32[2,304,256]{2,0,1:T(2,128)} async-done(((f32[2,304,256]{2,0,1:T(2,128)}), f32[2,304,256]{2,0,1:T(2,128)}) %all-reduce.33.cloned.1.call-update) | async-done | bytes 622608
  701.0 17.3 %all_gather.63 = bf16[2,304,256]{2,0,1:T(2,128)(2,1)S(1)} all-gather(bf16[2,19,256]{2,0,1:T(2,128)(2,1)S(1)} %dynamic-slice_convert_fusion.1), channel_id=1, replica_groups=mesh['row'=16,'col'=8] {'row'}, dimensions={1}, use_global_device_ids=true | all-gather | bytes 330752 | tf_op jit(solution)/shard_map/all_gather | solution.py:50
  720.5 62.6 %all-reduce.35.cloned.1.call-done = f32[1,152,256]{2,0,1:T(1,128)} async-done(((f32[1,152,256]{2,0,1:T(1,128)}), f32[1,152,256]{2,0,1:T(1,128)}) %all-reduce.35.cloned.1.call-update) | async-done | bytes 155664
  783.8 14.0 all_gather.64
  799.3 82.5 %all-reduce.44 = bf16[1,304,256]{2,0,1:T(2,128)(2,1)S(1)} all-reduce(f32[1,304,256]{2,0,1:T(1,128)S(1)} %copy.120), channel_id=10, replica_groups=mesh['row'=16,'col'=8] {'row'}, use_global_device_ids=true, to_apply=%region_18.0.clone | all-reduce | flops 77824 | bytes 466944
  881.8 16.1 all_gather.65
  899.0 28.1 %fusion = bf16[24,256]{1,0:T(8,128)(2,1)S(1)} fusion(bf16[1,152,256]{2,1,0:T(8,128)(2,1)S(1)} %fusion.58), kind=kCustom, calls=%all-reduce-scatter | all-reduce-scatter fusion | flops 49153 | bytes 90624
  927.2 1.9 collective-permute-start
  929.1 1.6 collective-permute-start.1
  931.8 13.8 all_gather.66
  947.9 81.9 %all-reduce.37.cloned.1.call-done = bf16[2,304,256]{2,0,1:T(2,128)(2,1)} async-done(((bf16[2,304,256]{2,0,1:T(2,128)(2,1)}), bf16[2,304,256]{2,0,1:T(2,128)(2,1)}) %all-reduce.37.cloned.1.call-update) | async-done | bytes 311312
  1030.6 17.3 %all_gather.68 = bf16[2,304,256]{2,0,1:T(2,128)(2,1)S(1)} all-gather(bf16[2,19,256]{2,0,1:T(2,128)(2,1)S(1)} %subtract_convert_fusion.4), channel_id=1, replica_groups=mesh['row'=16,'col'=8] {'row'}, dimensions={1}, use_global_device_ids=true | all-gather | bytes 330752 | tf_op jit(solution)/shard_map/all_gather | solution.py:83
  1049.9 62.6 %all-reduce.39.cloned.1.call-done = bf16[2,152,256]{2,0,1:T(2,128)(2,1)} async-done(((bf16[2,152,256]{2,0,1:T(2,128)(2,1)}), bf16[2,152,256]{2,0,1:T(2,128)(2,1)}) %all-reduce.39.cloned.1.call-update) | async-done | bytes 155664
  1113.2 14.0 all_gather.69
  1131.4 1.8 fusion.82
  1133.2 81.5 %all-reduce.41.cloned.1.call-done = bf16[4,304,256]{2,0,1:T(4,128)(2,1)} async-done(((bf16[4,304,256]{2,0,1:T(4,128)(2,1)}), bf16[4,304,256]{2,0,1:T(4,128)(2,1)}) %all-reduce.41.cloned.1.call-update) | async-done | bytes 622608
  1215.6 17.5 %all_gather.70 = bf16[4,304,256]{2,0,1:T(4,128)(2,1)S(1)} all-gather(bf16[4,19,256]{2,0,1:T(4,128)(2,1)S(1)} %subtract_convert_fusion.3), channel_id=1, replica_groups=mesh['row'=16,'col'=8] {'row'}, dimensions={1}, use_global_device_ids=true | all-gather | bytes 661504 | tf_op jit(solution)/shard_map/all_gather | solution.py:83
  1235.4 3.2 fusion.80
  1238.7 60.0 %all-reduce.43.cloned.1.call-done = bf16[4,152,256]{2,0,1:T(4,128)(2,1)} async-done(((bf16[4,152,256]{2,0,1:T(4,128)(2,1)}), bf16[4,152,256]{2,0,1:T(4,128)(2,1)}) %all-reduce.43.cloned.1.call-update) | async-done | bytes 311312
  1299.5 15.9 all_gather.71
  1315.4 3.0 fusion.44
  1320.0 70.7 %reduce-scatter.29.cloned.1.call-done = bf16[8,19,256]{2,0,1:T(8,128)(2,1)} async-done(((bf16[8,304,256]{2,0,1:T(8,128)(2,1)}), bf16[8,19,256]{2,0,1:T(8,128)(2,1)}) %reduce-scatter.29.cloned.1.call-update) | async-done | bytes 77840
  1392.3 43.6 %all-gather.12.cloned.1.call-done = bf16[8,304,256]{2,0,1:T(8,128)(2,1)} async-done(((bf16[8,19,256]{2,0,1:T(8,128)(2,1)}), bf16[8,304,256]{2,0,1:T(8,128)(2,1)}) %all-gather.12.cloned.1.call-update) | async-done | bytes 1245200 | tf_op jit(solution)/shard_map/all_gather | solution.py:83
  1435.9 2.1 fusion.48
  1438.9 4.8 fusion.10
  1443.8 4.8 fusion.8
  1448.7 4.7 fusion.6
  1453.4 15.0 reduce-scatter.21.cloned.1.call-done
  1468.4 16.9 %all_gather.73 = bf16[8,152,256]{2,0,1:T(8,128)(2,1)S(1)} all-gather(bf16[8,19,256]{2,0,1:T(8,128)(2,1)} %reduce-scatter.21.cloned.1.call-done), channel_id=1, replica_groups=mesh['row'=16,'col'=8] {'col'}, dimensions={1}, use_global_device_ids=true | all-gather | bytes 700416 | tf_op jit(solution)/shard_map/all_gather | solution.py:96
  1485.5 8.2 fusion.1
  1493.7 2.4 copy.137
  1496.1 72.9 %reduce-scatter.31.cloned.1.call-done = bf16[16,19,256]{2,0,1:T(8,128)(2,1)} async-done(((bf16[16,304,256]{2,0,1:T(8,128)(2,1)}), bf16[16,19,256]{2,0,1:T(8,128)(2,1)}) %reduce-scatter.31.cloned.1.call-update) | async-done | bytes 155664
  1569.0 1.6 subtract_convert_fusion
  1570.7 46.9 %all-gather.14.cloned.1.call-done = bf16[16,304,256]{2,0,1:T(8,128)(2,1)} async-done(((bf16[16,19,256]{2,0,1:T(8,128)(2,1)}), bf16[16,304,256]{2,0,1:T(8,128)(2,1)}) %all-gather.14.cloned.1.call-update) | async-done | bytes 2490384 | tf_op jit(solution)/shard_map/all_gather | solution.py:83
  1617.6 3.3 fusion.39
  1622.2 29.4 %reduce-scatter.23.cloned.1.call-done = bf16[16,19,256]{2,0,1:T(8,128)(2,1)} async-done(((bf16[16,152,256]{2,0,1:T(8,128)(2,1)}), bf16[16,19,256]{2,0,1:T(8,128)(2,1)}) %reduce-scatter.23.cloned.1.call-update) | async-done | bytes 155664 | tf_op jit(solution)/shard_map/reduce_scatter | solution.py:90
  (129 shorter events, 45.2 us)
Async XLA Ops:
  6.5 29.9 %all-gather.6.cloned.1.call-start = ((), (), s32[]{:S(2)}) async-start(), calls=%async_computation.7 | async-start | bytes 1400832 | tf_op jit(solution)/shard_map/all_gather | solution.py:39
  8.2 113.5 %reduce-scatter.25.cloned.1.call-start = ((), (), s32[]{:S(2)}) async-start(), calls=%async_computation.24 | async-start | bytes 5292032
  44.6 78.7 %copy-start.6 = (s32[98]{0:T(128)S(1)}, s32[98]{0:T(128)}, u32[]{:S(2)}) copy-start(s32[98]{0:T(128)} %param.11) | copy-start | bytes 1180
  44.7 125.4 %all-gather.8.cloned.1.call-start = ((), (), s32[]{:S(2)}) async-start(), calls=%async_computation.8 | async-start | bytes 2646016 | tf_op jit(solution)/shard_map/all_gather | solution.py:50
  123.3 81.1 %reduce-scatter.19.cloned.1.call-start = ((), (), s32[]{:S(2)}) async-start(), calls=%async_computation.9 | async-start | bytes 1400832 | tf_op jit(solution)/shard_map/reduce_scatter | solution.py:36
  173.6 30.8 %copy-start.2 = (bf16[31,19,256]{2,0,1:T(8,128)(2,1)S(1)}, bf16[31,19,256]{2,0,1:T(8,128)(2,1)}, u32[]{:S(2)}) copy-start(bf16[31,19,256]{2,0,1:T(8,128)(2,1)} %param.6) | copy-start | bytes 904708
  175.1 124.4 %reduce-scatter.27.cloned.1.call-start = ((), (), s32[]{:S(2)}) async-start(), calls=%async_computation.25 | async-start | bytes 2646016
  226.6 117.5 %all-gather.10.cloned.1.call-start = ((), (), s32[]{:S(2)}) async-start(), calls=%async_computation.10 | async-start | bytes 1323008 | tf_op jit(solution)/shard_map/all_gather | solution.py:50
  301.0 106.1 %all-reduce.27.cloned.1.call-start = ((), (), s32[]{:S(2)}) async-start(), calls=%async_computation.15 | async-start | bytes 1245184
  346.2 1.3 copy-start.4
  347.4 166.0 %all-reduce.29.cloned.1.call-start = ((), (), s32[]{:S(2)}) async-start(), calls=%async_computation.16 | async-start | bytes 2490368
  424.5 3.7 copy-start.7
  427.8 170.0 %all-reduce.31.cloned.1.call-start = ((), (), s32[]{:S(2)}) async-start(), calls=%async_computation.17 | async-start | bytes 622592
  429.4 3.5 copy-start.5
  534.1 166.1 %all-reduce.33.cloned.1.call-start = ((), (), s32[]{:S(2)}) async-start(), calls=%async_computation.18 | async-start | bytes 1245184
  616.9 166.1 %all-reduce.35.cloned.1.call-start = ((), (), s32[]{:S(2)}) async-start(), calls=%async_computation.19 | async-start | bytes 311296
  720.4 309.3 %all-reduce.37.cloned.1.call-start = ((), (), s32[]{:S(2)}) async-start(), calls=%async_computation.20 | async-start | bytes 622592
  927.2 4.3 collective-permute-start
  929.1 2.3 collective-permute-start.1
  947.8 164.7 %all-reduce.39.cloned.1.call-start = ((), (), s32[]{:S(2)}) async-start(), calls=%async_computation.21 | async-start | bytes 311296
  1049.8 164.9 %all-reduce.41.cloned.1.call-start = ((), (), s32[]{:S(2)}) async-start(), calls=%async_computation.22 | async-start | bytes 1245184
  1131.3 167.3 %all-reduce.43.cloned.1.call-start = ((), (), s32[]{:S(2)}) async-start(), calls=%async_computation.23 | async-start | bytes 622592
  1235.3 155.4 %reduce-scatter.29.cloned.1.call-start = ((), (), s32[]{:S(2)}) async-start(), calls=%async_computation.26 | async-start | bytes 1323008
  1318.4 72.3 %copy-start.1 = (f32[8,19,256]{2,0,1:T(8,128)S(1)}, f32[8,19,256]{2,0,1:T(8,128)}, u32[]{:S(2)}) copy-start(f32[8,19,256]{2,0,1:T(8,128)} %reduce-scatter.27.cloned.1.call-done) | copy-start | bytes 466948
  1319.9 115.9 %all-gather.12.cloned.1.call-start = ((), (), s32[]{:S(2)}) async-start(), calls=%async_computation.11 | async-start | bytes 1323008 | tf_op jit(solution)/shard_map/all_gather | solution.py:83
  1392.2 76.1 %reduce-scatter.21.cloned.1.call-start = ((), (), s32[]{:S(2)}) async-start(), calls=%async_computation.12 | async-start | bytes 700416 | tf_op jit(solution)/shard_map/reduce_scatter | solution.py:90
  1438.9 130.1 %reduce-scatter.31.cloned.1.call-start = ((), (), s32[]{:S(2)}) async-start(), calls=%async_computation.27 | async-start | bytes 2646016
  1496.0 73.0 %copy-start = (f32[16,19,256]{2,0,1:T(8,128)S(1)}, f32[16,19,256]{2,0,1:T(8,128)}, u32[]{:S(2)}) copy-start(f32[16,19,256]{2,0,1:T(8,128)} %reduce-scatter.25.cloned.1.call-done) | copy-start | bytes 933892
  1496.1 121.5 %all-gather.14.cloned.1.call-start = ((), (), s32[]{:S(2)}) async-start(), calls=%async_computation.13 | async-start | bytes 2646016 | tf_op jit(solution)/shard_map/all_gather | solution.py:83
  1570.6 80.9 %reduce-scatter.23.cloned.1.call-start = ((), (), s32[]{:S(2)}) async-start(), calls=%async_computation.14 | async-start | bytes 1400832 | tf_op jit(solution)/shard_map/reduce_scatter | solution.py:90
  1620.9 30.7 %copy-start.3 = (bf16[8,19,256]{2,0,1:T(8,128)(2,1)S(1)}, bf16[8,19,256]{2,0,1:T(8,128)(2,1)}, u32[]{:S(2)}) copy-start(bf16[8,19,256]{2,0,1:T(8,128)(2,1)} %reduce-scatter.21.cloned.1.call-done) | copy-start | bytes 233476
Sparse Core Ops, SparseCore 0:
  9.0 27.3 all-gather.5
  44.8 76.7 reduce-scatter.24
  123.7 46.3 all-gather.7
  175.2 29.1 reduce-scatter.18
  226.7 72.7 reduce-scatter.26
  301.5 42.5 all-gather.9
  347.5 59.5 all-reduce.26
  427.9 85.4 all-reduce.28
  534.2 63.5 all-reduce.30
  617.1 83.1 all-reduce.32
  720.5 62.4 all-reduce.34
  947.9 81.7 all-reduce.36
  1049.9 62.4 all-reduce.38
  1131.5 83.2 all-reduce.40
  1235.4 63.1 all-reduce.42
  1320.1 70.5 reduce-scatter.28
  1392.9 42.9 all-gather.11
  1439.0 29.3 reduce-scatter.20
  1496.2 72.7 reduce-scatter.30
  1571.2 46.3 all-gather.13
  1622.3 29.1 reduce-scatter.22
where the time goes:
time: 1670 us; the launch traced here: 1660 us
  waiting for transfers between devices  1200 us (72%)
  blocking collectives  319 us (19%)
  matrix products  75.6 us (5%)
  local copies, waits for them, and re-layouts  34.4 us (2%)
    unnamed x36, waiting for transfers between devices  920 us
    unnamed x2, blocking collectives  111 us
    all_gather x2, waiting for transfers between devices, on_device(): lax.all_gather(target.astype(jnp.bfloat16), 'row', axis=1, tiled=True)  90.5 us
    all_gather x2, waiting for transfers between devices, on_device(): lax.all_gather(solved_part.astype(jnp.bfloat16), 'row', axis=1, tiled=True)  86 us
    all_gather x4, blocking collectives, on_device(): lax.all_gather(target.astype(jnp.bfloat16), 'col', axis=1, tiled=True)  62.7 us
    all_gather x4, blocking collectives, on_device(): lax.all_gather(solved_part.astype(jnp.bfloat16), 'col', axis=1, tiled=True)  60.5 us
    all_gather x3, blocking collectives, on_device(): lax.all_gather(target.astype(jnp.bfloat16), 'row', axis=1, tiled=True)  50.9 us
    reduce_scatter x2, waiting for transfers between devices, on_device(): lax.psum_scatter(partial_value.astype(jnp.bfloat16), 'col', scatter_dimen...  44.3 us
  transfers between devices with their start and end apart: 23, of which 22 were waited for; matrix products, arithmetic and copies ran while one was open for 2% of the time, Pallas kernels for 0%

commit v1 on v0

v1 whole, which is shorter than its diff:
```python
import jax
import jax.numpy as jnp
import numpy as np
from jax import lax
from jax.experimental import pallas as pl
from jax.experimental.pallas import tpu as pltpu
from jax.sharding import PartitionSpec as P

LEVELS = 5
K = 31
NOFF = 98
R = 256
H = 128
TALL = 304
LOW = 152
PITCH = 160
SMALL = 19
PAIR = 48
MEMBERS = [16, 8, 4, 2, 1]
NODE = [0, 16, 24, 28, 30]
SLOT = [0, 64, 88, 96, 98]
PIECE = {16: 1216, 8: 608, 4: 304, 2: 160, 1: 80}
CHUNK = {16: 304, 8: 304, 4: 304, 2: 160, 1: 80}
FWROW = [0, 1216, 1824, 2128, 2288]
FWROWS = 2368
MESH = pl.DeviceIdType.MESH
BF = jnp.bfloat16
F32 = jnp.float32

RS, EX, AG, CR, CG, YX, IY, IC, FC, FY = 0, 6, 12, 18, 19, 20, 26, 32, 34, 35
NSEM = 38


def placing():
    put = np.zeros((2, LOW, 8 * PAIR), np.float32)
    for r in range(LOW):
        c, i = divmod(r, SMALL)
        at = ((c % 2) * 4 + c // 2) * PAIR + i
        put[0, r, at] = 1
        put[1, r, at + SMALL] = 1
    return put, np.swapaxes(put, 1, 2)


def dot(a, b):
    return jnp.dot(a, b, preferred_element_type=F32)


def kernel(
    rs, put, take, present, linv, loff, uinv, uoff, out,
    pb, rb, es, eb, xb, fw, tot, cb, crb, ct, ys, yb, lowb, rg, ag0, ag1, sp, crs, fys, fyr,
    ssem, rsem, wsem,
):
    row, col = lax.axis_index("row"), lax.axis_index("col")
    z, x = row // 4, row % 4
    y, core = col // 2, col % 2
    sibling = (row, y * 2 + 1 - core)
    along = (z, x)

    def zpeer(d):
        return (((z + d) % 4) * 4 + x, col)

    def xpeer(d):
        return (z * 4 + (x + d) % 4, col)

    def ypeer(d):
        return (row, ((y + d) % 4) * 2 + core)

    first_peer = (zpeer, xpeer)
    second_peer = (xpeer, zpeer)

    barrier = pltpu.get_barrier_semaphore()
    for d in (1, 2, 3):
        for peer in (zpeer, xpeer, ypeer):
            pl.semaphore_signal(barrier, inc=1, device_id=peer(d), device_id_type=MESH)
    pl.semaphore_signal(barrier, inc=1, device_id=sibling, device_id_type=MESH)
    pl.semaphore_wait(barrier, 10)

    def send(src, dst, sem, to):
        c = pltpu.make_async_remote_copy(
            src, dst, ssem.at[sem], rsem.at[sem], device_id=to, device_id_type=MESH
        )
        c.start()
        return c

    def wait(copies):
        for c in copies:
            c.wait()

    def chunks(rows, chunk, body):
        if rows == chunk:
            body(pl.ds(0, chunk), 0)
        else:

            def step(i, _):
                at = pl.multiple_of(i * chunk, 16)
                body(pl.ds(at, chunk), at)
                return 0

            lax.fori_loop(0, rows // chunk, step, 0)

    def each(n, body):
        if n <= 2:
            for i in range(n):
                body(i)
        else:

            def step(i, _):
                body(i)
                return 0

            lax.fori_loop(0, n, step, 0)

    def tall_get(ref, m, j):
        if m >= 4:
            per = m // 4
            q, at = j // per, (j % per) * TALL
            if not isinstance(at, int):
                at = pl.multiple_of(at, 16)
            halves = [ref[h, q, pl.ds(at, TALL), :] for h in (0, 1)]
        elif m == 2:
            halves = [
                jnp.concatenate([ref[h, 2 * j, 0:160, :], ref[h, 2 * j + 1, 0:144, :]], axis=0)
                for h in (0, 1)
            ]
        else:
            halves = [
                jnp.concatenate(
                    [ref[h, q, 0:80, :] for q in range(3)] + [ref[h, 3, 0:64, :]], axis=0
                )
                for h in (0, 1)
            ]
        return jnp.concatenate(halves, axis=1)

    def tall_put(ref, m, j, value):
        value = value.astype(BF)
        for h in (0, 1):
            v = value[:, h * H : (h + 1) * H]
            if m >= 4:
                per = m // 4
                q, at = j // per, (j % per) * TALL
                if not isinstance(at, int):
                    at = pl.multiple_of(at, 16)
                ref[h, q, pl.ds(at, TALL), :] = v
            elif m == 2:
                ref[h, 2 * j, 0:160, :] = v[0:160]
                ref[h, 2 * j + 1, 0:144, :] = v[160:304]
            else:
                for q in range(3):
                    ref[h, q, 0:80, :] = v[80 * q : 80 * q + 80]
                ref[h, 3, 0:64, :] = v[240:304]

    def low_rows(j):
        at = j * PITCH
        return pl.ds(at if isinstance(at, int) else pl.multiple_of(at, 16), LOW)

    def low_get(ref, j):
        return jnp.concatenate([ref[h, low_rows(j), :] for h in (0, 1)], axis=1)

    def low_put(ref, j, value):
        value = value.astype(BF)
        for h in (0, 1):
            ref[h, low_rows(j), :] = value[:, h * H : (h + 1) * H]

    def row_start(rows):
        return [
            [
                send(
                    pb.at[h, (along[h] + d) % 4, pl.ds(0, rows)],
                    rb.at[h, d - 1, pl.ds(0, rows)],
                    RS + h * 3 + d - 1,
                    first_peer[h](d),
                )
                for d in (2, 1, 3)
            ]
            for h in (0, 1)
        ]

    def row_finish(copies, level, forward, aside=None):
        m = MEMBERS[level]
        rows, chunk, base = PIECE[m], CHUNK[m], FWROW[level]
        second = []
        for h in (0, 1):
            wait(copies[h])

            def add(at, _, h=h):
                s = pb[h, along[h], at, :].astype(F32)
                for k in range(3):
                    s = s + rb[h, k, at, :].astype(F32)
                tot[h, at, :] = s
                es[h, at, :] = s.astype(BF)

            chunks(rows, chunk, add)
            second.append(
                [
                    send(
                        es.at[h, pl.ds(0, rows)],
                        eb.at[h, d - 1, pl.ds(0, rows)],
                        EX + h * 3 + d - 1,
                        second_peer[h](d),
                    )
                    for d in (2, 1, 3)
                ]
            )
        if aside is not None:
            aside()
        third = []
        for h in (0, 1):
            wait(second[h])

            def last(at, start, h=h):
                s = tot[h, at, :]
                for k in range(3):
                    s = s + eb[h, k, at, :].astype(F32)
                kept = pl.ds(
                    base + start if isinstance(start, int) else pl.multiple_of(base + start, 16),
                    chunk,
                )
                if forward:
                    fw[h, kept, :] = s
                else:
                    s = fw[h, kept, :] - s
                xb[h, along[h], at, :] = s.astype(BF)

            chunks(rows, chunk, last)
            mine = xb.at[h, along[h], pl.ds(0, rows)]
            third.append(
                [send(mine, mine, AG + h * 3 + d - 1, first_peer[h](d)) for d in (2, 1, 3)]
            )
        for h in (0, 1):
            wait(third[h])

    def col_reduce(m, turn, base=None, aside=None):
        rows = m * PITCH
        wait([send(cb.at[1 - core, pl.ds(0, rows)], crb.at[pl.ds(0, rows)], CR, sibling)])

        def add(at, _):
            s = cb[core, at, :].astype(F32) + crb[at, :].astype(F32)
            ct[at, :] = s
            ys[at, :] = s.astype(BF)

        chunks(rows, PITCH, add)
        copies = [
            send(
                ys.at[pl.ds(0, rows)],
                yb.at[turn, d - 1, pl.ds(0, rows)],
                YX + turn * 3 + d - 1,
                ypeer(d),
            )
            for d in (2, 1, 3)
        ]
        if aside is not None:
            aside()
        wait(copies)

        def last(at, start):
            s = ct[at, :]
            for k in range(3):
                s = s + yb[turn, k, at, :].astype(F32)
            if base is not None:
                first = base + start
                if not isinstance(start, int):
                    first = pl.multiple_of(first, 16)
                s = rg[core, pl.ds(first, PITCH), :].astype(F32) - s
            lowb[core, at, :] = s.astype(BF)

        chunks(rows, PITCH, last)
        mine = lowb.at[core, pl.ds(0, rows)]
        wait([send(mine, mine, CG, sibling)])

    def gather_y(part, buf):
        return [
            send(rs.at[part], buf.at[core, y], IY + part * 3 + d - 1, ypeer(d)) for d in (2, 1, 3)
        ]

    def unpack(buf, pairs, into, single_last):
        def one(p):
            at = p * PAIR
            if not isinstance(at, int):
                at = pl.multiple_of(at, 16)
            v = buf[:, :, pl.ds(at, PAIR), :].reshape(8 * PAIR, R)
            for e in (0, 1):
                low_put(into, 2 * p + e, dot(put[e], v))

        each(pairs - 1 if single_last else pairs, one)
        if single_last:
            p = pairs - 1
            v = buf[:, :, pl.ds(p * PAIR, PAIR), :].reshape(8 * PAIR, R)
            low_put(into, 2 * p, dot(put[0], v))

    turn = 0

    def fetch(src, dst, first, n, sem):
        c = pltpu.make_async_copy(src.at[pl.ds(first, n)], dst.at[pl.ds(first, n)], wsem.at[sem])
        c.start()
        return c

    def forward_sweep(li, lo, waiting):
        inv_copy, off_copy = [], []
        ic0 = gather_y(0, ag0)
        ic1 = gather_y(1, ag1)
        for level in range(LEVELS):
            inv_copy.append(fetch(linv, li, NODE[level], MEMBERS[level], level))
            if level < 4:
                off_copy.append(
                    fetch(loff, lo, SLOT[level], SLOT[level + 1] - SLOT[level], 5 + level)
                )
        ag0[core, y] = rs[0]
        ag1[core, y] = rs[1]
        wait(ic0)
        wait([send(ag0.at[core], ag0.at[core], IC, sibling)])
        unpack(ag0, 8, lowb, False)
        turn = 0
        for level in range(LEVELS):
            m = MEMBERS[level]
            above = LEVELS - 1 - level
            inv_copy[level].wait()
            each(m, lambda j: tall_put(pb, m, j, dot(li[NODE[level] + j], low_get(lowb, j))))
            copies = row_start(PIECE[m])
            if level == 0:
                wait(ic1)
                wait([send(ag1.at[core], ag1.at[core], IC + 1, sibling)])
                unpack(ag1, 8, rg, True)
                waiting[...] = jnp.zeros_like(waiting)
            row_finish(copies, level, True)
            if above == 0:
                break
            off_copy[level].wait()

            def product(j, a):
                slot = SLOT[level] + j * above + a - 1
                scale = present[slot].astype(F32)
                return scale * dot(lo[slot], tall_get(xb, m, j))

            def near(t):
                value = product(2 * t, 1) + product(2 * t + 1, 1)
                if level > 0:
                    value = value + waiting[NODE[level + 1] - 16 + t]
                low_put(cb, t, value)

            each(m // 2, near)

            def far():
                def one(j):
                    for a in range(2, above + 1):
                        t = NODE[level + a] - 16 + j // 2**a
                        waiting[t] = waiting[t] + product(j, a)

                each(m, one)

            col_reduce(
                m // 2, turn, (NODE[level + 1] - 16) * PITCH, far if above > 1 else None
            )
            turn = 1 - turn

    pl.run_scoped(
        forward_sweep,
        pltpu.VMEM((K, TALL, LOW), BF),
        pltpu.VMEM((NOFF, LOW, TALL), BF),
        pltpu.VMEM((15, LOW, R), F32),
    )

    def backward_sweep(ui, uo, upward):
        inv_copy, off_copy = {}, {}
        for level in reversed(range(LEVELS)):
            if level < 4:
                off_copy[level] = fetch(
                    uoff, uo, SLOT[level], SLOT[level + 1] - SLOT[level], 5 + level
                )
            inv_copy[level] = fetch(uinv, ui, NODE[level], MEMBERS[level], level)
        turn = 0
        for level in reversed(range(1, LEVELS)):
            m = MEMBERS[level]
            inv_copy[level].wait()
            each(m, lambda j: low_put(cb, j, dot(ui[NODE[level] + j], tall_get(xb, m, j))))
            col_reduce(m, turn)
            turn = 1 - turn
            if level == 4:
                off_copy[3].wait()

            def product(j, a):
                under = level - a
                slot = SLOT[under] + j * (LEVELS - 1 - under) + a - 1
                scale = present[slot].astype(F32)
                return scale * dot(uo[slot], low_get(lowb, j // 2**a))

            def near(j):
                value = product(j, 1)
                if level < 4:
                    value = value + upward[NODE[level - 1] + j]
                tall_put(pb, 2 * m, j, value)

            each(2 * m, near)
            copies = row_start(PIECE[2 * m])
            for a in range(2, level + 1):
                under = level - a
                if level == 4:
                    off_copy[under].wait()

                def far(j, a=a, under=under):
                    value = product(j, a)
                    if level < 4:
                        value = value + upward[NODE[under] + j]
                    upward[NODE[under] + j] = value

                each(MEMBERS[under], far)
            own = pl.ds(pl.multiple_of((core * 4 + y) * PAIR, 16), PAIR)
            if m == 1:
                out[15] = dot(take[0, own, :], low_get(lowb, 0))
            else:

                def show(p):
                    out[NODE[level] // 2 + p] = dot(
                        take[0, own, :], low_get(lowb, 2 * p)
                    ) + dot(take[1, own, :], low_get(lowb, 2 * p + 1))

                each(m // 2, show)
            row_finish(copies, level - 1, False)

        inv_copy[0].wait()

        def leaf(p):
            at = pl.multiple_of(p * PAIR, 16)
            v = [
                dot(ui[2 * p + e], tall_get(xb, 16, 2 * p + e)).astype(BF) for e in (0, 1)
            ]
            s = dot(take[0], v[0]) + dot(take[1], v[1])
            sp[:, :, pl.ds(at, PAIR), :] = s.astype(BF).reshape(2, 4, PAIR, R)

        each(8, leaf)
        wait([send(sp.at[1 - core], crs, FC, sibling)])
        copies = []
        for d in (2, 1, 3):
            to = (y + d) % 4

            def add(at, _, to=to):
                fys[to, at, :] = (
                    sp[core, to, at, :].astype(F32) + crs[to, at, :].astype(F32)
                ).astype(BF)

            chunks(8 * PAIR, 2 * PAIR, add)
            copies.append(send(fys.at[to], fyr.at[d - 1], FY + d - 1, ypeer(d)))
        wait(copies)

        def finish(p):
            at = pl.ds(pl.multiple_of(p * PAIR, 16), PAIR)
            s = sp[core, y, at, :].astype(F32) + crs[y, at, :].astype(F32)
            for k in range(3):
                s = s + fyr[k, at, :].astype(F32)
            out[p] = s

        each(8, finish)

    pl.run_scoped(
        backward_sweep,
        pltpu.VMEM((K, LOW, TALL), BF),
        pltpu.VMEM((NOFF, TALL, LOW), BF),
        pltpu.VMEM((30, TALL, R), F32),
    )


def on_device(right_sides, lower_inv, lower_off, upper_inv, upper_off, present):
    shares = jnp.pad(right_sides, ((0, 1), (0, 0), (0, 0))).reshape(16, 2 * SMALL, R)
    shares = jnp.pad(shares, ((0, 0), (0, PAIR - 2 * SMALL), (0, 0))).reshape(2, 8 * PAIR, R)
    put, take = placing()
    vmem = pl.BlockSpec(memory_space=pltpu.VMEM)
    hbm = pl.BlockSpec(memory_space=pl.ANY)
    out = pl.pallas_call(
        kernel,
        out_shape=jax.ShapeDtypeStruct((16, PAIR, R), F32),
        in_specs=[vmem, vmem, vmem, pl.BlockSpec(memory_space=pltpu.SMEM), hbm, hbm, hbm, hbm],
        out_specs=vmem,
        scratch_shapes=[
            pltpu.VMEM((2, 4, 1216, H), BF),
            pltpu.VMEM((2, 3, 1216, H), BF),
            pltpu.VMEM((2, 1216, H), BF),
            pltpu.VMEM((2, 3, 1216, H), BF),
            pltpu.VMEM((2, 4, 1216, H), BF),
            pltpu.VMEM((2, FWROWS, H), F32),
            pltpu.VMEM((2, 1216, H), F32),
            pltpu.VMEM((2, 8 * PITCH, H), BF),
            pltpu.VMEM((8 * PITCH, H), BF),
            pltpu.VMEM((8 * PITCH, H), F32),
            pltpu.VMEM((8 * PITCH, H), BF),
            pltpu.VMEM((2, 3, 8 * PITCH, H), BF),
            pltpu.VMEM((2, 16 * PITCH, H), BF),
            pltpu.VMEM((2, 15 * PITCH, H), BF),
            pltpu.VMEM((2, 4, 8 * PAIR, R), BF),
            pltpu.VMEM((2, 4, 8 * PAIR, R), BF),
            pltpu.VMEM((2, 4, 8 * PAIR, R), BF),
            pltpu.VMEM((4, 8 * PAIR, R), BF),
            pltpu.VMEM((4, 8 * PAIR, R), BF),
            pltpu.VMEM((3, 8 * PAIR, R), BF),
            pltpu.SemaphoreType.DMA((NSEM,)),
            pltpu.SemaphoreType.DMA((NSEM,)),
            pltpu.SemaphoreType.DMA((9,)),
        ],
        compiler_params=pltpu.CompilerParams(
            collective_id=0, has_side_effects=True, vmem_limit_bytes=60 * 1024 * 1024
        ),
    )(
        shares,
        jnp.asarray(put, BF),
        jnp.asarray(take, BF),
        present,
        lower_inv,
        lower_off,
        upper_inv,
        upper_off,
    )
    return out[:, : 2 * SMALL].reshape(32, SMALL, R)[:K]


def solution(mesh):
    placed = (
        P(None, ("row", "col"), None),
        P(None, "col", "row"),
        P(None, "row", "col"),
        P(None, "row", "col"),
        P(None, "col", "row"),
        P(),
    )
    return jax.shard_map(
        on_device,
        mesh=mesh,
        in_specs=placed,
        out_specs=P(None, ("row", "col"), None),
        check_vma=False,
    )
```

time: 1670 us -> 410 us (0.25)
  waiting for transfers between devices: 1200 us -> 0 us
  Pallas kernels: 0 us -> 379 us
  blocking collectives: 319 us -> 0 us
  matrix products: 75.6 us -> 0 us
    unnamed x36 -> x0, waiting for transfers between devices: 920 us -> none
    pallas_call x0 -> x1, Pallas kernels: none -> 379 us  [on_device(): pl.pallas_call(kernel, out_shape=jax.ShapeDtypeStruct((16, PAIR, R), F32)...]
    all_gather x13 -> x0, blocking collectives: 209 us -> none  [the longest x4 62.7 us: on_device(): lax.all_gather(target.astype(jnp.bfloat16), 'col', axis=1, tiled=True)]
    all_gather x5 -> x0, waiting for transfers between devices: 205 us -> none  [the longest x2 90.5 us: on_device(): lax.all_gather(target.astype(jnp.bfloat16), 'row', axis=1, tiled=True)]
    unnamed x2 -> x0, blocking collectives: 111 us -> none
    dot_general x30 -> x0, matrix products: 75.6 us -> none  [the longest x10 34.7 us: on_device(): jnp.einsum('oal,olp->oap', block_list, repeated_copies, preferred_element...]
    reduce_scatter x3 -> x0, waiting for transfers between devices: 73.6 us -> none  [the longest x2 44.3 us: on_device(): lax.psum_scatter(partial_value.astype(jnp.bfloat16), 'col', scatter_dimen...]
    unnamed x24 -> x3, local copies, waits for them, and re-layouts: 3.09 us -> 26.3 us
  transfers between devices with their start and end apart: 23 -> 0, of which waited for: 22 -> 0; matrix products, arithmetic and copies ran while one was open for 2% -> 0% of each run, Pallas kernels for 0% -> 0%
where the time goes in v1:
time: 410 us; the launch traced here: 409 us
  Pallas kernels  379 us (92%)
  local copies, waits for them, and re-layouts  29.5 us (7%)
    pallas_call x1, Pallas kernels, on_device(): pl.pallas_call(kernel, out_shape=jax.ShapeDtypeStruct((16, PAIR, R), F32)...  379 us
    unnamed x3, local copies, waits for them, and re-layouts  26.3 us

profile of v1, /device:TPU:1, one launch (start us, length us, event | category | flops | bytes accessed | tf_op | source)
XLA Modules:
  0.0 409.0 jit_solution(760123633355501889)
XLA Ops:
  0.0 1.1 copy.16
  1.2 0.1 reshape.9
  1.3 0.8 pad.9
  2.0 6.9 %copy.13.linv = bf16[31,304,152]{2,1,0:T(8,128)(2,1)} copy(bf16[31,304,152]{1,2,0:T(8,128)(2,1)} %param.9) | data formatting | bytes 5729792 | tf_op args[1]
  9.0 18.2 %copy.14.uoff = bf16[98,304,152]{2,1,0:T(8,128)(2,1)} copy(bf16[98,304,152]{1,2,0:T(8,128)(2,1)} %param.12) | data formatting | bytes 18113536 | tf_op args[4]
  27.2 379.5 %shard_map.82 = f32[16,48,256]{2,1,0:T(8,128)} custom-call(bf16[2,384,256]{2,1,0:T(8,128)(2,1)} %bitcast.1, bf16[2,152,384]{2,1,0:T(8,128)(2,1)} %constant.7.clone.put, bf16[2,384,152]{2,1,0:T(8,128)(2,1)} %constant.8.clone.take, s32[98]{0:T(128)} %present.1, bf16[31,304,152]{2,1,0:T(8,128)(2,1)} %copy.13.linv, bf16[98,152,304]{2,1,0:T(8,128)(2,1)} %loff.1, ...), custom_call_target="tpu_custom_call" | custom-call | tf_op jit(solution)/shard_map/pallas_call | solution.py:467
  406.7 1.1 slice.6
  407.8 0.1 reshape.11
  407.9 0.1 slice.8
  408.0 1.0 copy.15
  (1 shorter events, 0.0 us)

commit v2 on v1

v2 whole, which is shorter than its diff:
```python
import jax
import jax.numpy as jnp
from jax import lax
from jax.experimental import pallas as pl
from jax.experimental.pallas import tpu as pltpu
from jax.sharding import PartitionSpec as P

LEVELS = 5
K = 31
NOFF = 98
R = 256
H = 128
TALL = 304
LOW = 152
PITCH = 160
SMALL = 19
SHARES = 304
MEMBERS = [16, 8, 4, 2, 1]
NODE = [0, 16, 24, 28, 30]
SLOT = [0, 64, 88, 96, 98]
PIECE = {8: 608, 4: 304, 2: 160, 1: 80}
FWROW = [0, 608, 912, 1072, 1152]
FWROWS = 1232
MESH = pl.DeviceIdType.MESH
BF = jnp.bfloat16
F32 = jnp.float32

RS, EX, AG, CR, CG, YX, HALF = 0, 6, 12, 18, 19, 20, 26
IY, IC, FC, FY = 52, 64, 68, 70
NSEM = 76


def dot(a, b):
    return jnp.dot(a, b, preferred_element_type=F32)


def dot_first(a, b):
    return lax.dot_general(a, b, (((0,), (0,)), ((), ())), preferred_element_type=F32)


def kernel(
    rs, present, linv, loff, uinv, uoff, out,
    pb, rb, es, eb, xb, fw, tot, cb, crb, ct, ys, yb, lowb, rg, ag0, ag1, wide, shown, sp, crs, fys, fyr,
    ssem, rsem, wsem,
):
    row, col = lax.axis_index("row"), lax.axis_index("col")
    z, x = row // 4, row % 4
    y, core = col // 2, col % 2
    sibling = (row, y * 2 + 1 - core)
    along = (z, x)

    def zpeer(d):
        return (((z + d) % 4) * 4 + x, col)

    def xpeer(d):
        return (z * 4 + (x + d) % 4, col)

    def ypeer(d):
        return (row, ((y + d) % 4) * 2 + core)

    first_peer = (zpeer, xpeer)
    second_peer = (xpeer, zpeer)

    for h in (0, 1):
        part = slice(h * H, (h + 1) * H)
        ag0[h, y, core] = rs[:, 0:16, part]
        ag1[h, y, core] = jnp.concatenate(
            [rs[:, 16:31, part], jnp.zeros((SMALL, 1, H), BF)], axis=1
        )

    barrier = pltpu.get_barrier_semaphore()
    for d in (1, 2, 3):
        for peer in (zpeer, xpeer, ypeer):
            pl.semaphore_signal(barrier, inc=1, device_id=peer(d), device_id_type=MESH)
    pl.semaphore_signal(barrier, inc=1, device_id=sibling, device_id_type=MESH)
    pl.semaphore_wait(barrier, 10)

    def send(src, dst, sem, to):
        c = pltpu.make_async_remote_copy(
            src, dst, ssem.at[sem], rsem.at[sem], device_id=to, device_id_type=MESH
        )
        c.start()
        return c

    def wait(copies):
        for c in copies:
            c.wait()

    def chunks(rows, chunk, body):
        if rows == chunk:
            body(pl.ds(0, chunk), 0)
        else:

            def step(i, _):
                at = pl.multiple_of(i * chunk, 16)
                body(pl.ds(at, chunk), at)
                return 0

            lax.fori_loop(0, rows // chunk, step, 0)

    def each(n, body):
        if n <= 2:
            for i in range(n):
                body(i)
        else:

            def step(i, _):
                body(i)
                return 0

            lax.fori_loop(0, n, step, 0)

    def tall_get(ref, m, j):
        if m >= 4:
            per = m // 4
            q, at = j // per, (j % per) * TALL
            if not isinstance(at, int):
                at = pl.multiple_of(at, 16)
            halves = [ref[h, q, pl.ds(at, TALL), :] for h in (0, 1)]
        elif m == 2:
            halves = [
                jnp.concatenate([ref[h, 2 * j, 0:160, :], ref[h, 2 * j + 1, 0:144, :]], axis=0)
                for h in (0, 1)
            ]
        else:
            halves = [
                jnp.concatenate(
                    [ref[h, q, 0:80, :] for q in range(3)] + [ref[h, 3, 0:64, :]], axis=0
                )
                for h in (0, 1)
            ]
        return jnp.concatenate(halves, axis=1)

    def tall_put(ref, m, j, value):
        value = value.astype(BF)
        for h in (0, 1):
            v = value[:, h * H : (h + 1) * H]
            if m >= 4:
                per = m // 4
                q, at = j // per, (j % per) * TALL
                if not isinstance(at, int):
                    at = pl.multiple_of(at, 16)
                ref[h, q, pl.ds(at, TALL), :] = v
            elif m == 2:
                ref[h, 2 * j, 0:160, :] = v[0:160]
                ref[h, 2 * j + 1, 0:144, :] = v[160:304]
            else:
                for q in range(3):
                    ref[h, q, 0:80, :] = v[80 * q : 80 * q + 80]
                ref[h, 3, 0:64, :] = v[240:304]

    def low_rows(j):
        at = j * PITCH
        return pl.ds(at if isinstance(at, int) else pl.multiple_of(at, 16), LOW)

    def low_get(ref, j):
        return jnp.concatenate([ref[h, low_rows(j), :] for h in (0, 1)], axis=1)

    def low_put(ref, j, value):
        value = value.astype(BF)
        for h in (0, 1):
            ref[h, low_rows(j), :] = value[:, h * H : (h + 1) * H]

    def row_reduce(t, m, level, forward):
        rows, base, sem = PIECE[m], FWROW[level], HALF * t
        chunk = min(rows, TALL)
        first = [
            [
                send(
                    pb.at[t, h, (along[h] + d) % 4, pl.ds(0, rows)],
                    rb.at[t, h, d - 1, pl.ds(0, rows)],
                    sem + RS + h * 3 + d - 1,
                    first_peer[h](d),
                )
                for d in (2, 1, 3)
            ]
            for h in (0, 1)
        ]
        yield
        second = []
        for h in (0, 1):
            wait(first[h])

            def add(at, _, h=h):
                s = pb[t, h, along[h], at, :].astype(F32)
                for k in range(3):
                    s = s + rb[t, h, k, at, :].astype(F32)
                tot[t, h, at, :] = s
                es[t, h, at, :] = s.astype(BF)

            chunks(rows, chunk, add)
            second.append(
                [
                    send(
                        es.at[t, h, pl.ds(0, rows)],
                        eb.at[t, h, d - 1, pl.ds(0, rows)],
                        sem + EX + h * 3 + d - 1,
                        second_peer[h](d),
                    )
                    for d in (2, 1, 3)
                ]
            )
        yield
        third = []
        for h in (0, 1):
            wait(second[h])

            def last(at, start, h=h):
                s = tot[t, h, at, :]
                for k in range(3):
                    s = s + eb[t, h, k, at, :].astype(F32)
                kept = pl.ds(
                    base + start if isinstance(start, int) else pl.multiple_of(base + start, 16),
                    chunk,
                )
                if forward:
                    fw[t, h, kept, :] = s
                else:
                    s = fw[t, h, kept, :] - s
                xb[t, h, along[h], at, :] = s.astype(BF)

            chunks(rows, chunk, last)
            mine = xb.at[t, h, along[h], pl.ds(0, rows)]
            third.append(
                [send(mine, mine, sem + AG + h * 3 + d - 1, first_peer[h](d)) for d in (2, 1, 3)]
            )
        yield
        for h in (0, 1):
            wait(third[h])

    turns = [0, 0]

    def col_reduce(t, m, base=None, aside=None):
        rows, sem, turn = m * PITCH, HALF * t, turns[t]
        turns[t] = 1 - turn
        copies = [
            send(cb.at[t, 1 - core, pl.ds(0, rows)], crb.at[t, pl.ds(0, rows)], sem + CR, sibling)
        ]
        yield
        wait(copies)

        def add(at, _):
            s = cb[t, core, at, :].astype(F32) + crb[t, at, :].astype(F32)
            ct[t, at, :] = s
            ys[t, at, :] = s.astype(BF)

        chunks(rows, PITCH, add)
        copies = [
            send(
                ys.at[t, pl.ds(0, rows)],
                yb.at[t, turn, d - 1, pl.ds(0, rows)],
                sem + YX + turn * 3 + d - 1,
                ypeer(d),
            )
            for d in (2, 1, 3)
        ]
        if aside is not None:
            aside()
        yield
        wait(copies)

        def last(at, start):
            s = ct[t, at, :]
            for k in range(3):
                s = s + yb[t, turn, k, at, :].astype(F32)
            if base is not None:
                first = base + start
                if not isinstance(start, int):
                    first = pl.multiple_of(first, 16)
                s = rg[core, pl.ds(first, PITCH), :].astype(F32) - s
            lowb[t, core, at, :] = s.astype(BF)

        chunks(rows, PITCH, last)
        mine = lowb.at[t, core, pl.ds(0, rows)]
        copies = [send(mine, mine, sem + CG, sibling)]
        yield
        wait(copies)

    def gather_y(part, buf):
        return [
            [
                send(
                    buf.at[h, y, core],
                    buf.at[h, y, core],
                    IY + part * 6 + h * 3 + d - 1,
                    ypeer(d),
                )
                for d in (2, 1, 3)
            ]
            for h in (0, 1)
        ]

    def gather_core(part, buf, copies):
        more = []
        for h in (0, 1):
            wait(copies[h])
            mine = buf.at[h, :, core]
            more.append(send(mine, mine, IC + part * 2 + h, sibling))
        return more

    def unpack(copies, buf, members, place):
        for h in (0, 1):
            wait([copies[h]])
            for c in range(8):
                v = buf[h, c // 2, c % 2].astype(F32).reshape(SHARES, H)
                wide[h, pl.ds(c * SHARES, SHARES), :] = v
            for j in range(members):
                v = wide[h, pl.ds(j, LOW, stride=16), :]
                place(h, j, v.astype(BF))

    def col_steps(*args):
        for _ in col_reduce(*args):
            yield 1

    def row_steps(*args):
        for _ in row_reduce(*args):
            yield 1

    def run(halves):
        halves = list(halves)
        while halves:
            for g in list(halves):
                if next(g, 0) == 0:
                    halves.remove(g)

    def fetch(src, dst, first, n, sem):
        c = pltpu.make_async_copy(src.at[pl.ds(first, n)], dst.at[pl.ds(first, n)], wsem.at[sem])
        c.start()
        return c

    def forward_sweep(li, lo, waiting):
        inv_copy, off_copy = [], []
        ic0 = gather_y(0, ag0)
        ic1 = gather_y(1, ag1)
        for level in range(LEVELS):
            inv_copy.append(fetch(linv, li, NODE[level], MEMBERS[level], level))
            if level < 4:
                off_copy.append(
                    fetch(loff, lo, SLOT[level], SLOT[level + 1] - SLOT[level], 5 + level)
                )
        waiting[...] = jnp.zeros_like(waiting)

        def leaves(h, j, v):
            lowb[j // 8, h, low_rows(j % 8), :] = v

        def others(h, j, v):
            rg[h, low_rows(j), :] = v

        def solve(t, m, level):
            first = NODE[level] + t * m

            def one(j):
                tall_put(pb.at[t], m, j, dot_first(li[first + j], low_get(lowb.at[t], j)))

            each(m, one)

        def product(t, m, level, j, a):
            above = LEVELS - 1 - level
            slot = SLOT[level] + (t * m + j) * above + a - 1
            scale = present[slot].astype(F32)
            return scale * dot(lo[slot], tall_get(xb.at[t], m, j))

        def half(t):
            for level in range(4):
                m = MEMBERS[level] // 2
                above = LEVELS - 1 - level
                if t == 0:
                    inv_copy[level].wait()
                solve(t, m, level)
                for _ in row_reduce(t, m, level, True):
                    yield 1
                if t == 0:
                    off_copy[level].wait()
                if level == 3:
                    break
                to = NODE[level + 1] - 16 + t * (m // 2)

                def near(k, level=level, m=m, to=to):
                    value = product(t, m, level, 2 * k, 1) + product(t, m, level, 2 * k + 1, 1)
                    if level > 0:
                        value = value + waiting[to + k]
                    low_put(cb.at[t], k, value)

                each(m // 2, near)

                def far(level=level, m=m, above=above):
                    def one(j):
                        for a in range(2, above + 1):
                            k = NODE[level + a] - 16 + (t * m + j) // 2**a
                            waiting[k] = waiting[k] + product(t, m, level, j, a)

                    each(m, one)

                for _ in col_reduce(t, m // 2, to * PITCH, far):
                    yield 1

        unpack(gather_core(0, ag0, ic0), ag0, 16, leaves)
        halves = [half(0), half(1)]
        for g in halves:
            next(g)
        unpack(gather_core(1, ag1, ic1), ag1, 15, others)
        run(halves)
        low_put(cb.at[0], 0, waiting[14] + product(0, 1, 3, 0, 1) + product(1, 1, 3, 0, 1))
        run([col_steps(0, 1, 14 * PITCH)])
        inv_copy[4].wait()
        solve(0, 1, 4)
        run([row_steps(0, 1, 4, True)])

    pl.run_scoped(
        forward_sweep,
        pltpu.VMEM((K, LOW, TALL), BF),
        pltpu.VMEM((NOFF, LOW, TALL), BF),
        pltpu.VMEM((15, LOW, R), F32),
    )

    def backward_sweep(ui, uo, upward):
        spot = lax.broadcasted_iota(jnp.int32, (24, LOW), 1)
        at_row = lax.broadcasted_iota(jnp.int32, (24, LOW), 0) + col * SMALL
        own = jnp.where(spot == at_row, 1.0, 0.0).astype(BF)
        inv_copy, off_copy = {}, {}
        for level in reversed(range(LEVELS)):
            if level < 4:
                off_copy[level] = fetch(
                    uoff, uo, SLOT[level], SLOT[level + 1] - SLOT[level], 5 + level
                )
            inv_copy[level] = fetch(uinv, ui, NODE[level], MEMBERS[level], level)

        def solve(t, m, level):
            first = NODE[level] + t * m

            def one(j):
                low_put(cb.at[t], j, dot(ui[first + j], tall_get(xb.at[t], m, j)))

            each(m, one)

        def product(t, level, under, j, k):
            slot = SLOT[under] + j * (LEVELS - 1 - under) + level - under - 1
            scale = present[slot].astype(F32)
            return scale * dot_first(uo[slot], low_get(lowb.at[t], k))

        def show(t, m, level):
            for j in range(m):
                v = dot(own, low_get(lowb.at[t], j))[:SMALL]
                for h in (0, 1):
                    shown[h, pl.ds(NODE[level] - 16 + t * m + j, SMALL, stride=16), :] = v[
                        :, h * H : (h + 1) * H
                    ]

        inv_copy[4].wait()
        solve(0, 1, 4)
        run([col_steps(0, 1)])
        off_copy[3].wait()
        for t in (0, 1):
            tall_put(pb.at[t], 1, 0, product(0, 4, 3, t, 0))

        def half(t):
            for _ in row_reduce(t, 1, 3, False):
                yield 1
            for level in (3, 2, 1):
                m = MEMBERS[level] // 2
                if t == 0:
                    inv_copy[level].wait()
                solve(t, m, level)
                for _ in col_reduce(t, m):
                    yield 1

                def near(i, level=level, m=m):
                    j = t * 2 * m + i
                    value = product(t, level, level - 1, j, i // 2)
                    tall_put(pb.at[t], 2 * m, i, value + upward[NODE[level - 1] + j])

                each(2 * m, near)
                steps = row_reduce(t, 2 * m, level - 1, False)
                next(steps)
                for under in range(level - 2, -1, -1):

                    def far(i, level=level, m=m, under=under):
                        j = t * (MEMBERS[under] // 2) + i
                        value = product(t, level, under, j, i // 2 ** (level - under))
                        upward[NODE[under] + j] = value + upward[NODE[under] + j]

                    each(MEMBERS[under] // 2, far)
                show(t, m, level)
                yield 1
                for _ in steps:
                    yield 1

        halves = [half(0), half(1)]
        for g in halves:
            next(g)
        for under in (2, 1, 0):
            off_copy[under].wait()

            def root_far(j, under=under):
                upward[NODE[under] + j] = product(0, 4, under, j, 0)

            each(MEMBERS[under], root_far)
        show(0, 1, 4)
        run(halves)

        inv_copy[0].wait()
        for j in range(16):
            v = dot(ui[j], tall_get(xb.at[j // 8], 8, j % 8))
            for h in (0, 1):
                wide[h, pl.ds(j, LOW, stride=16), :] = v[:, h * H : (h + 1) * H]
        first = []
        for h in (0, 1):
            for c in range(8):
                sp[h, c // 2, c % 2] = wide[h, pl.ds(c * SHARES, SHARES), :].astype(BF)
            first.append(send(sp.at[h, :, 1 - core], crs.at[h], FC + h, sibling))
        second = []
        for h in (0, 1):
            wait([first[h]])
            copies = []
            for d in (2, 1, 3):
                to = (y + d) % 4
                fys[h, to] = (sp[h, to, core].astype(F32) + crs[h, to].astype(F32)).astype(BF)
                copies.append(send(fys.at[h, to], fyr.at[h, d - 1], FY + h * 3 + d - 1, ypeer(d)))
            second.append(copies)

        def move(i):
            at = pl.ds(pl.multiple_of(i * 16, 16), 16)
            to = pl.ds(pl.multiple_of(i * 32 + 16, 16), 16)
            for h in (0, 1):
                out[to, h * H : (h + 1) * H] = shown[h, at, :]

        each(SMALL, move)
        for h in (0, 1):
            wait(second[h])

            def finish(i, h=h):
                at = pl.ds(pl.multiple_of(i * 16, 16), 16)
                s = sp[h, y, core, at, :].astype(F32) + crs[h, y, at, :].astype(F32)
                for k in range(3):
                    s = s + fyr[h, k, at, :].astype(F32)
                out[pl.ds(pl.multiple_of(i * 32, 32), 16), h * H : (h + 1) * H] = s

            each(SMALL, finish)

    pl.run_scoped(
        backward_sweep,
        pltpu.VMEM((K, LOW, TALL), BF),
        pltpu.VMEM((NOFF, LOW, TALL), BF),
        pltpu.VMEM((30, TALL, R), F32),
    )


def on_device(right_sides, lower_inv, lower_off, upper_inv, upper_off, present):
    vmem = pl.BlockSpec(memory_space=pltpu.VMEM)
    hbm = pl.BlockSpec(memory_space=pl.ANY)
    out = pl.pallas_call(
        kernel,
        out_shape=jax.ShapeDtypeStruct((32 * SMALL, R), F32),
        in_specs=[vmem, pl.BlockSpec(memory_space=pltpu.SMEM), hbm, hbm, hbm, hbm],
        out_specs=vmem,
        scratch_shapes=[
            pltpu.VMEM((2, 2, 4, 608, H), BF),
            pltpu.VMEM((2, 2, 3, 608, H), BF),
            pltpu.VMEM((2, 2, 608, H), BF),
            pltpu.VMEM((2, 2, 3, 608, H), BF),
            pltpu.VMEM((2, 2, 4, 608, H), BF),
            pltpu.VMEM((2, 2, FWROWS, H), F32),
            pltpu.VMEM((2, 2, 608, H), F32),
            pltpu.VMEM((2, 2, 4 * PITCH, H), BF),
            pltpu.VMEM((2, 4 * PITCH, H), BF),
            pltpu.VMEM((2, 4 * PITCH, H), F32),
            pltpu.VMEM((2, 4 * PITCH, H), BF),
            pltpu.VMEM((2, 2, 3, 4 * PITCH, H), BF),
            pltpu.VMEM((2, 2, 8 * PITCH, H), BF),
            pltpu.VMEM((2, 15 * PITCH, H), BF),
            pltpu.VMEM((2, 4, 2, SMALL, 16, H), BF),
            pltpu.VMEM((2, 4, 2, SMALL, 16, H), BF),
            pltpu.VMEM((2, 8 * SHARES, H), F32),
            pltpu.VMEM((2, SHARES, H), F32),
            pltpu.VMEM((2, 4, 2, SHARES, H), BF),
            pltpu.VMEM((2, 4, SHARES, H), BF),
            pltpu.VMEM((2, 4, SHARES, H), BF),
            pltpu.VMEM((2, 3, SHARES, H), BF),
            pltpu.SemaphoreType.DMA((NSEM,)),
            pltpu.SemaphoreType.DMA((NSEM,)),
            pltpu.SemaphoreType.DMA((9,)),
        ],
        compiler_params=pltpu.CompilerParams(
            collective_id=0, has_side_effects=True, vmem_limit_bytes=60 * 1024 * 1024
        ),
    )(
        jnp.swapaxes(right_sides, 0, 1),
        present,
        jnp.swapaxes(lower_inv, 1, 2),
        lower_off,
        upper_inv,
        jnp.swapaxes(upper_off, 1, 2),
    )
    return jnp.swapaxes(out.reshape(SMALL, 32, R)[:, :K], 0, 1)


def solution(mesh):
    placed = (
        P(None, ("row", "col"), None),
        P(None, "col", "row"),
        P(None, "row", "col"),
        P(None, "row", "col"),
        P(None, "col", "row"),
        P(),
    )
    return jax.shard_map(
        on_device,
        mesh=mesh,
        in_specs=placed,
        out_specs=P(None, ("row", "col"), None),
        check_vma=False,
    )
```

time: 410 us -> 325 us (0.79)
  Pallas kernels: 379 us -> 323 us
  local copies, waits for them, and re-layouts: 29.5 us -> 1.96 us
    pallas_call x1, Pallas kernels: 379 us -> 323 us  [on_device(): pl.pallas_call(kernel, out_shape=jax.ShapeDtypeStruct((32 * SMALL, R), F3...]
    unnamed x3 -> x0, local copies, waits for them, and re-layouts: 26.3 us -> none
where the time goes in v2:
time: 325 us
  Pallas kernels  323 us (99%)
    pallas_call x1, Pallas kernels, on_device(): pl.pallas_call(kernel, out_shape=jax.ShapeDtypeStruct((32 * SMALL, R), F3...  323 us

profile of v2, /device:TPU:1, one launch (start us, length us, event | category | flops | bytes accessed | tf_op | source)
XLA Modules:
  0.0 324.7 jit_solution(16573085538346615851)
XLA Ops:
  0.0 322.8 %shard_map.64 = f32[608,256]{1,0:T(8,128)} custom-call(bf16[19,31,256]{2,1,0:T(8,128)(2,1)} %bitcast.9, s32[98]{0:T(128)} %present.1, bf16[31,152,304]{2,1,0:T(8,128)(2,1)} %bitcast.7, bf16[98,152,304]{2,1,0:T(8,128)(2,1)} %loff.1, bf16[31,152,304]{2,1,0:T(8,128)(2,1)} %uinv.1, bf16[98,152,304]{2,1,0:T(8,128)(2,1)} %bitcast.6), custom_call_target="tpu_custom_call" | custom-call | tf_op jit(solution)/shard_map/pallas_call | solution.py:551
  322.8 2.0 slice_bitcast_fusion

commit v3 on v2

--- a/solution.py
+++ b/solution.py
@@ -40,7 +40,7 @@
 
 def kernel(
     rs, present, linv, loff, uinv, uoff, out,
-    pb, rb, es, eb, xb, fw, tot, cb, crb, ct, ys, yb, lowb, rg, ag0, ag1, wide, shown, sp, crs, fys, fyr,
+    pb, rb, es, eb, xb, fw, tot, cb, crb, ct, ys, yb, lowb, topb, rg, ag0, ag1, wide, shown, sp, crs, fys, fyr,
     ssem, rsem, wsem,
 ):
     row, col = lax.axis_index("row"), lax.axis_index("col")
@@ -108,7 +108,7 @@
                 body(i)
                 return 0
 
-            lax.fori_loop(0, n, step, 0)
+            lax.fori_loop(0, n, step, 0, unroll=2 if n % 2 == 0 else 1)
 
     def tall_get(ref, m, j):
         if m >= 4:
@@ -255,6 +255,7 @@
             for d in (2, 1, 3)
         ]
         if aside is not None:
+            yield
             aside()
         yield
         wait(copies)
@@ -472,6 +473,7 @@
                 each(2 * m, near)
                 steps = row_reduce(t, 2 * m, level - 1, False)
                 next(steps)
+                yield 1
                 for under in range(level - 2, -1, -1):
 
                     def far(i, level=level, m=m, under=under):
@@ -484,25 +486,41 @@
                 yield 1
                 for _ in steps:
                     yield 1
+            if t == 0:
+                inv_copy[0].wait()
+            for j in range(8):
+                v = dot(ui[t * 8 + j], tall_get(xb.at[t], 8, j))
+                for h in (0, 1):
+                    wide[h, pl.ds(t * 8 + j, LOW, stride=16), :] = v[:, h * H : (h + 1) * H]
 
         halves = [half(0), half(1)]
         for g in halves:
             next(g)
-        for under in (2, 1, 0):
-            off_copy[under].wait()
-
-            def root_far(j, under=under):
-                upward[NODE[under] + j] = product(0, 4, under, j, 0)
-
-            each(MEMBERS[under], root_far)
+        for h in (0, 1):
+            topb[h, :, :] = lowb[0, h, 0:PITCH, :]
+
+        def root_part(under, first, n):
+            def one(i):
+                j = first + i
+                slot = SLOT[under] + j * (LEVELS - 1 - under) + 3 - under
+                scale = present[slot].astype(F32)
+                upward[NODE[under] + j] = scale * dot_first(uo[slot], low_get(topb, 0))
+
+            each(n, one)
+
+        def root_far():
+            for under in (2, 1, 0):
+                off_copy[under].wait()
+                for first in range(0, MEMBERS[under], 4):
+                    root_part(under, first, 4)
+                    if (under, first) != (0, 12):
+                        if (under, first) != (0, 8):
+                            yield 1
+            yield 1
+
         show(0, 1, 4)
-        run(halves)
-
-        inv_copy[0].wait()
-        for j in range(16):
-            v = dot(ui[j], tall_get(xb.at[j // 8], 8, j % 8))
-            for h in (0, 1):
-                wide[h, pl.ds(j, LOW, stride=16), :] = v[:, h * H : (h + 1) * H]
+        run(halves + [root_far()])
+
         first = []
         for h in (0, 1):
             for c in range(8):
@@ -567,6 +585,7 @@
             pltpu.VMEM((2, 4 * PITCH, H), BF),
             pltpu.VMEM((2, 2, 3, 4 * PITCH, H), BF),
             pltpu.VMEM((2, 2, 8 * PITCH, H), BF),
+            pltpu.VMEM((2, PITCH, H), BF),
             pltpu.VMEM((2, 15 * PITCH, H), BF),
             pltpu.VMEM((2, 4, 2, SMALL, 16, H), BF),
             pltpu.VMEM((2, 4, 2, SMALL, 16, H), BF),

time: 325 us -> 319 us (0.982)
  Pallas kernels: 323 us -> 317 us
    pallas_call x1, Pallas kernels: 323 us -> 317 us  [on_device(): pl.pallas_call(kernel, out_shape=jax.ShapeDtypeStruct((32 * SMALL, R), F3...]
where the time goes in v3:
time: 319 us
  Pallas kernels  317 us (99%)
    pallas_call x1, Pallas kernels, on_device(): pl.pallas_call(kernel, out_shape=jax.ShapeDtypeStruct((32 * SMALL, R), F3...  317 us

profile of v3, /device:TPU:1, one launch (start us, length us, event | category | flops | bytes accessed | tf_op | source)
XLA Modules:
  0.0 318.5 jit_solution(15094635039536972479)
XLA Ops:
  0.0 316.5 %shard_map.64 = f32[608,256]{1,0:T(8,128)} custom-call(bf16[19,31,256]{2,1,0:T(8,128)(2,1)} %bitcast.9, s32[98]{0:T(128)} %present.1, bf16[31,152,304]{2,1,0:T(8,128)(2,1)} %bitcast.7, bf16[98,152,304]{2,1,0:T(8,128)(2,1)} %loff.1, bf16[31,152,304]{2,1,0:T(8,128)(2,1)} %uinv.1, bf16[98,152,304]{2,1,0:T(8,128)(2,1)} %bitcast.6), custom_call_target="tpu_custom_call" | custom-call | tf_op jit(solution)/shard_map/pallas_call | solution.py:569
  316.6 2.0 slice_bitcast_fusion

commit v4 on v3

--- a/solution.py
+++ b/solution.py
@@ -14,7 +14,7 @@
 LOW = 152
 PITCH = 160
 SMALL = 19
-SHARES = 304
+GROUP = 152
 MEMBERS = [16, 8, 4, 2, 1]
 NODE = [0, 16, 24, 28, 30]
 SLOT = [0, 64, 88, 96, 98]
@@ -26,8 +26,8 @@
 F32 = jnp.float32
 
 RS, EX, AG, CR, CG, YX, HALF = 0, 6, 12, 18, 19, 20, 26
-IY, IC, FC, FY = 52, 64, 68, 70
-NSEM = 76
+IY, IC, FC, FY = 52, 76, 84, 88
+NSEM = 100
 
 
 def dot(a, b):
@@ -40,7 +40,7 @@
 
 def kernel(
     rs, present, linv, loff, uinv, uoff, out,
-    pb, rb, es, eb, xb, fw, tot, cb, crb, ct, ys, yb, lowb, topb, rg, ag0, ag1, wide, shown, sp, crs, fys, fyr,
+    pb, rb, es, eb, xb, fw, tot, cb, crb, ct, ys, yb, lowb, topb, rg, ag, wide, shown, sp, crs, fys, fyr,
     ssem, rsem, wsem,
 ):
     row, col = lax.axis_index("row"), lax.axis_index("col")
@@ -63,10 +63,11 @@
 
     for h in (0, 1):
         part = slice(h * H, (h + 1) * H)
-        ag0[h, y, core] = rs[:, 0:16, part]
-        ag1[h, y, core] = jnp.concatenate(
-            [rs[:, 16:31, part], jnp.zeros((SMALL, 1, H), BF)], axis=1
-        )
+        ends = jnp.concatenate([rs[:, 16:31, part], jnp.zeros((SMALL, 1, H), BF)], axis=1)
+        for g in range(4):
+            v = (rs[:, 0:16, part] if g < 2 else ends).astype(F32)
+            v = v[:, 8 * (g % 2) : 8 * (g % 2) + 8, :].reshape(GROUP, H)
+            ag[g, h, y, core, 0:GROUP, :] = v.astype(BF)
 
     barrier = pltpu.get_barrier_semaphore()
     for d in (1, 2, 3):
@@ -277,13 +278,13 @@
         yield
         wait(copies)
 
-    def gather_y(part, buf):
+    def gather_y(g):
         return [
             [
                 send(
-                    buf.at[h, y, core],
-                    buf.at[h, y, core],
-                    IY + part * 6 + h * 3 + d - 1,
+                    ag.at[g, h, y, core],
+                    ag.at[g, h, y, core],
+                    IY + g * 6 + h * 3 + d - 1,
                     ypeer(d),
                 )
                 for d in (2, 1, 3)
@@ -291,22 +292,23 @@
             for h in (0, 1)
         ]
 
-    def gather_core(part, buf, copies):
+    def gather_core(g, copies):
         more = []
         for h in (0, 1):
             wait(copies[h])
-            mine = buf.at[h, :, core]
-            more.append(send(mine, mine, IC + part * 2 + h, sibling))
+            mine = ag.at[g, h, :, core]
+            more.append(send(mine, mine, IC + g * 2 + h, sibling))
         return more
 
-    def unpack(copies, buf, members, place):
+    def unpack(g, copies, members, place):
+        t = g % 2
         for h in (0, 1):
             wait([copies[h]])
             for c in range(8):
-                v = buf[h, c // 2, c % 2].astype(F32).reshape(SHARES, H)
-                wide[h, pl.ds(c * SHARES, SHARES), :] = v
+                v = ag[g, h, c // 2, c % 2, 0:GROUP, :].astype(F32)
+                wide[t, h, pl.ds(c * GROUP, GROUP), :] = v
             for j in range(members):
-                v = wide[h, pl.ds(j, LOW, stride=16), :]
+                v = wide[t, h, pl.ds(j, LOW, stride=8), :]
                 place(h, j, v.astype(BF))
 
     def col_steps(*args):
@@ -331,8 +333,7 @@
 
     def forward_sweep(li, lo, waiting):
         inv_copy, off_copy = [], []
-        ic0 = gather_y(0, ag0)
-        ic1 = gather_y(1, ag1)
+        gathers = [gather_y(g) for g in range(4)]
         for level in range(LEVELS):
             inv_copy.append(fetch(linv, li, NODE[level], MEMBERS[level], level))
             if level < 4:
@@ -341,12 +342,6 @@
                 )
         waiting[...] = jnp.zeros_like(waiting)
 
-        def leaves(h, j, v):
-            lowb[j // 8, h, low_rows(j % 8), :] = v
-
-        def others(h, j, v):
-            rg[h, low_rows(j), :] = v
-
         def solve(t, m, level):
             first = NODE[level] + t * m
 
@@ -362,6 +357,10 @@
             return scale * dot(lo[slot], tall_get(xb.at[t], m, j))
 
         def half(t):
+            def leaves(h, j, v):
+                lowb[t, h, low_rows(j), :] = v
+
+            unpack(t, gather_core(t, gathers[t]), 8, leaves)
             for level in range(4):
                 m = MEMBERS[level] // 2
                 above = LEVELS - 1 - level
@@ -395,11 +394,15 @@
                 for _ in col_reduce(t, m // 2, to * PITCH, far):
                     yield 1
 
-        unpack(gather_core(0, ag0, ic0), ag0, 16, leaves)
         halves = [half(0), half(1)]
         for g in halves:
             next(g)
-        unpack(gather_core(1, ag1, ic1), ag1, 15, others)
+        for g in (2, 3):
+
+            def others(h, j, v, g=g):
+                rg[h, low_rows(8 * (g - 2) + j), :] = v
+
+            unpack(g, gather_core(g, gathers[g]), 8 if g == 2 else 7, others)
         run(halves)
         low_put(cb.at[0], 0, waiting[14] + product(0, 1, 3, 0, 1) + product(1, 1, 3, 0, 1))
         run([col_steps(0, 1, 14 * PITCH)])
@@ -491,7 +494,46 @@
             for j in range(8):
                 v = dot(ui[t * 8 + j], tall_get(xb.at[t], 8, j))
                 for h in (0, 1):
-                    wide[h, pl.ds(t * 8 + j, LOW, stride=16), :] = v[:, h * H : (h + 1) * H]
+                    wide[t, h, pl.ds(j, LOW, stride=8), :] = v[:, h * H : (h + 1) * H]
+            first = []
+            for h in (0, 1):
+                for c in range(8):
+                    v = wide[t, h, pl.ds(c * GROUP, GROUP), :]
+                    sp[t, h, c // 2, c % 2, 0:GROUP, :] = v.astype(BF)
+                first.append(
+                    send(sp.at[t, h, :, 1 - core], crs.at[t, h], FC + t * 2 + h, sibling)
+                )
+            yield 1
+            second = []
+            for h in (0, 1):
+                wait([first[h]])
+                copies = []
+                for d in (2, 1, 3):
+                    to = (y + d) % 4
+                    v = sp[t, h, to, core].astype(F32) + crs[t, h, to].astype(F32)
+                    fys[t, h, to] = v.astype(BF)
+                    copies.append(
+                        send(
+                            fys.at[t, h, to],
+                            fyr.at[t, h, d - 1],
+                            FY + t * 6 + h * 3 + d - 1,
+                            ypeer(d),
+                        )
+                    )
+                second.append(copies)
+            yield 1
+            if t == 0:
+                for i in range(SMALL):
+                    for h in (0, 1):
+                        v = shown[h, pl.ds(i * 16, 16), :]
+                        out[pl.ds(i * 32 + 16, 16), h * H : (h + 1) * H] = v
+            for h in (0, 1):
+                wait(second[h])
+                v = sp[t, h, y, core].astype(F32) + crs[t, h, y].astype(F32)
+                for k in range(3):
+                    v = v + fyr[t, h, k].astype(F32)
+                for i in range(SMALL):
+                    out[pl.ds(i * 32 + t * 8, 8), h * H : (h + 1) * H] = v[8 * i : 8 * i + 8]
 
         halves = [half(0), half(1)]
         for g in halves:
@@ -520,40 +562,6 @@
 
         show(0, 1, 4)
         run(halves + [root_far()])
-
-        first = []
-        for h in (0, 1):
-            for c in range(8):
-                sp[h, c // 2, c % 2] = wide[h, pl.ds(c * SHARES, SHARES), :].astype(BF)
-            first.append(send(sp.at[h, :, 1 - core], crs.at[h], FC + h, sibling))
-        second = []
-        for h in (0, 1):
-            wait([first[h]])
-            copies = []
-            for d in (2, 1, 3):
-                to = (y + d) % 4
-                fys[h, to] = (sp[h, to, core].astype(F32) + crs[h, to].astype(F32)).astype(BF)
-                copies.append(send(fys.at[h, to], fyr.at[h, d - 1], FY + h * 3 + d - 1, ypeer(d)))
-            second.append(copies)
-
-        def move(i):
-            at = pl.ds(pl.multiple_of(i * 16, 16), 16)
-            to = pl.ds(pl.multiple_of(i * 32 + 16, 16), 16)
-            for h in (0, 1):
-                out[to, h * H : (h + 1) * H] = shown[h, at, :]
-
-        each(SMALL, move)
-        for h in (0, 1):
-            wait(second[h])
-
-            def finish(i, h=h):
-                at = pl.ds(pl.multiple_of(i * 16, 16), 16)
-                s = sp[h, y, core, at, :].astype(F32) + crs[h, y, at, :].astype(F32)
-                for k in range(3):
-                    s = s + fyr[h, k, at, :].astype(F32)
-                out[pl.ds(pl.multiple_of(i * 32, 32), 16), h * H : (h + 1) * H] = s
-
-            each(SMALL, finish)
 
     pl.run_scoped(
         backward_sweep,
@@ -587,14 +595,13 @@
             pltpu.VMEM((2, 2, 8 * PITCH, H), BF),
             pltpu.VMEM((2, PITCH, H), BF),
             pltpu.VMEM((2, 15 * PITCH, H), BF),
-            pltpu.VMEM((2, 4, 2, SMALL, 16, H), BF),
-            pltpu.VMEM((2, 4, 2, SMALL, 16, H), BF),
-            pltpu.VMEM((2, 8 * SHARES, H), F32),
-            pltpu.VMEM((2, SHARES, H), F32),
-            pltpu.VMEM((2, 4, 2, SHARES, H), BF),
-            pltpu.VMEM((2, 4, SHARES, H), BF),
-            pltpu.VMEM((2, 4, SHARES, H), BF),
-            pltpu.VMEM((2, 3, SHARES, H), BF),
+            pltpu.VMEM((4, 2, 4, 2, PITCH, H), BF),
+            pltpu.VMEM((2, 2, 8 * GROUP + 16, H), F32),
+            pltpu.VMEM((2, 25 * 16, H), F32),
+            pltpu.VMEM((2, 2, 4, 2, PITCH, H), BF),
+            pltpu.VMEM((2, 2, 4, PITCH, H), BF),
+            pltpu.VMEM((2, 2, 4, PITCH, H), BF),
+            pltpu.VMEM((2, 2, 3, PITCH, H), BF),
             pltpu.SemaphoreType.DMA((NSEM,)),
             pltpu.SemaphoreType.DMA((NSEM,)),
             pltpu.SemaphoreType.DMA((9,)),

time: 319 us -> 314 us (0.984)
  Pallas kernels: 317 us -> 312 us
    pallas_call x1, Pallas kernels: 317 us -> 312 us  [on_device(): pl.pallas_call(kernel, out_shape=jax.ShapeDtypeStruct((32 * SMALL, R), F3...]
where the time goes in v4:
time: 314 us
  Pallas kernels  312 us (99%)
    pallas_call x1, Pallas kernels, on_device(): pl.pallas_call(kernel, out_shape=jax.ShapeDtypeStruct((32 * SMALL, R), F3...  312 us

profile of v4, /device:TPU:1, one launch (start us, length us, event | category | flops | bytes accessed | tf_op | source)
XLA Modules:
  0.0 313.6 jit_solution(2553158000952732633)
XLA Ops:
  0.0 311.6 %shard_map.64 = f32[608,256]{1,0:T(8,128)} custom-call(bf16[19,31,256]{2,1,0:T(8,128)(2,1)} %bitcast.9, s32[98]{0:T(128)} %present.1, bf16[31,152,304]{2,1,0:T(8,128)(2,1)} %bitcast.7, bf16[98,152,304]{2,1,0:T(8,128)(2,1)} %loff.1, bf16[31,152,304]{2,1,0:T(8,128)(2,1)} %uinv.1, bf16[98,152,304]{2,1,0:T(8,128)(2,1)} %bitcast.6), custom_call_target="tpu_custom_call" | custom-call | tf_op jit(solution)/shard_map/pallas_call | solution.py:577
  311.6 2.0 slice_bitcast_fusion

commit v5 on v4

--- a/solution.py
+++ b/solution.py
@@ -109,7 +109,7 @@
                 body(i)
                 return 0
 
-            lax.fori_loop(0, n, step, 0, unroll=2 if n % 2 == 0 else 1)
+            lax.fori_loop(0, n, step, 0, unroll=4 if n % 4 == 0 else 1)
 
     def tall_get(ref, m, j):
         if m >= 4:

time: 314 us -> 310 us (0.987)
  Pallas kernels: 312 us -> 308 us
    pallas_call x1, Pallas kernels: 312 us -> 308 us  [on_device(): pl.pallas_call(kernel, out_shape=jax.ShapeDtypeStruct((32 * SMALL, R), F3...]
where the time goes in v5:
time: 310 us
  Pallas kernels  308 us (99%)
    pallas_call x1, Pallas kernels, on_device(): pl.pallas_call(kernel, out_shape=jax.ShapeDtypeStruct((32 * SMALL, R), F3...  308 us

profile of v5, /device:TPU:1, one launch (start us, length us, event | category | flops | bytes accessed | tf_op | source)
XLA Modules:
  0.0 310.2 jit_solution(10111707081317815005)
XLA Ops:
  0.0 308.2 %shard_map.64 = f32[608,256]{1,0:T(8,128)} custom-call(bf16[19,31,256]{2,1,0:T(8,128)(2,1)} %bitcast.9, s32[98]{0:T(128)} %present.1, bf16[31,152,304]{2,1,0:T(8,128)(2,1)} %bitcast.7, bf16[98,152,304]{2,1,0:T(8,128)(2,1)} %loff.1, bf16[31,152,304]{2,1,0:T(8,128)(2,1)} %uinv.1, bf16[98,152,304]{2,1,0:T(8,128)(2,1)} %bitcast.6), custom_call_target="tpu_custom_call" | custom-call | tf_op jit(solution)/shard_map/pallas_call | solution.py:577
  308.2 2.0 slice_bitcast_fusion

commit v6 on v5

--- a/solution.py
+++ b/solution.py
@@ -99,7 +99,7 @@
 
             lax.fori_loop(0, rows // chunk, step, 0)
 
-    def each(n, body):
+    def each(n, body, unroll=8):
         if n <= 2:
             for i in range(n):
                 body(i)
@@ -109,7 +109,7 @@
                 body(i)
                 return 0
 
-            lax.fori_loop(0, n, step, 0, unroll=4 if n % 4 == 0 else 1)
+            lax.fori_loop(0, n, step, 0, unroll=min(n, unroll))
 
     def tall_get(ref, m, j):
         if m >= 4:
@@ -389,7 +389,7 @@
                             k = NODE[level + a] - 16 + (t * m + j) // 2**a
                             waiting[k] = waiting[k] + product(t, m, level, j, a)
 
-                    each(m, one)
+                    each(m, one, 2)
 
                 for _ in col_reduce(t, m // 2, to * PITCH, far):
                     yield 1
@@ -484,7 +484,7 @@
                         value = product(t, level, under, j, i // 2 ** (level - under))
                         upward[NODE[under] + j] = value + upward[NODE[under] + j]
 
-                    each(MEMBERS[under] // 2, far)
+                    each(MEMBERS[under] // 2, far, 2)
                 show(t, m, level)
                 yield 1
                 for _ in steps:
@@ -548,7 +548,7 @@
                 scale = present[slot].astype(F32)
                 upward[NODE[under] + j] = scale * dot_first(uo[slot], low_get(topb, 0))
 
-            each(n, one)
+            each(n, one, 2)
 
         def root_far():
             for under in (2, 1, 0):

time: 310 us -> 312 us (level)
  no operation moved by 1% of the time
where the time goes in v6:
time: 312 us
  Pallas kernels  310 us (99%)
    pallas_call x1, Pallas kernels, on_device(): pl.pallas_call(kernel, out_shape=jax.ShapeDtypeStruct((32 * SMALL, R), F3...  310 us

profile of v6, /device:TPU:1, one launch (start us, length us, event | category | flops | bytes accessed | tf_op | source)
XLA Modules:
  0.0 311.7 jit_solution(15237832521600325283)
XLA Ops:
  0.0 309.7 %shard_map.64 = f32[608,256]{1,0:T(8,128)} custom-call(bf16[19,31,256]{2,1,0:T(8,128)(2,1)} %bitcast.9, s32[98]{0:T(128)} %present.1, bf16[31,152,304]{2,1,0:T(8,128)(2,1)} %bitcast.7, bf16[98,152,304]{2,1,0:T(8,128)(2,1)} %loff.1, bf16[31,152,304]{2,1,0:T(8,128)(2,1)} %uinv.1, bf16[98,152,304]{2,1,0:T(8,128)(2,1)} %bitcast.6), custom_call_target="tpu_custom_call" | custom-call | tf_op jit(solution)/shard_map/pallas_call | solution.py:577
  309.7 2.0 slice_bitcast_fusion
